TPU v7x, 32 devices: a whole 2x2x4 slice. The times are simulated.
32 devices in a mesh: groups: 2 (over x), expert: 16 (over z, y, core).
Axes of the slice: x: 2, y: 2, z: 4, core: 2. Of those that a mesh axis runs over, the one named last changes fastest.
Arguments:
- tokens: bfloat16 [4096, 4096], P(('groups', 'expert')), parts along dimension 0, may hold values from -6 to 6
- grad_out: bfloat16 [4096, 4096], P(('groups', 'expert')), parts along dimension 0, may hold values from -0.09375 to 0.09375
- expert_ids: int32 [4096, 8], P(('groups', 'expert')), parts along dimension 0, may hold values from 0 to 127, all different within a row; in each aligned block of 128 rows (0 to 127, 128 to 255, ...) at most 10 rows name the same one
- route_weight: int32 [4096, 8], P(('groups', 'expert')), parts along dimension 0, may hold values from 1 to 256
- block_expert: int32 [16], replicated, may hold values from 0 to 1, as said below
- gate_blocks: bfloat16 [16, 4096, 128], P('expert'), may hold values from -0.09375 to 0.09375
- up_blocks: bfloat16 [16, 4096, 128], P('expert'), may hold values from -0.09375 to 0.09375
- down_blocks: bfloat16 [16, 128, 4096], P('expert'), may hold values from -0.1875 to 0.1875
Outputs:
- grad_gate: bfloat16 [32, 4096, 128], P(('groups', 'expert')), parts along dimension 0
- grad_up: bfloat16 [32, 4096, 128], P(('groups', 'expert')), parts along dimension 0
- grad_down: bfloat16 [32, 128, 4096], P(('groups', 'expert')), parts along dimension 0
- route_grad: float32 [4096, 8], P(('groups', 'expert')), parts along dimension 0
There are 2 independent parts, one for each index of `groups`. A program takes and returns all parts, laid end to end along the dimension named above; an argument that names none is the same for every part. Nothing has to cross between parts.
Inputs may be any that keep to these rules, and one draw needn't show every extreme that they name: `expert_ids`: in the rows of one device no expert is named more than 10 times. `block_expert`: each of the experts 0 to 1 holds 4 to 12 blocks; no other expert holds any.
All inputs are finite; a program needn't handle non-finite values.
Results may differ from a plain program's by a relative error of at most 0.0057.
Values may be sent and summed in bfloat16 or wider, within the bound.
A program may use at most 192 MiB of HBM per device.

v0:
```python
import jax
import jax.numpy as jnp
from jax import lax
from jax.sharding import PartitionSpec as P

EXPERTS = 128
CAP = 10


def forward_part(rows_x, joined_w, blk_width):
    joined = jnp.dot(rows_x, joined_w, preferred_element_type=jnp.float32)
    pre_gate = joined[:, :blk_width]
    pre_up = joined[:, blk_width:]
    sigma = jax.nn.sigmoid(pre_gate)
    hidden = (pre_gate * sigma * pre_up).astype(jnp.bfloat16)
    return (pre_gate, pre_up, sigma, hidden)


def backward_part(rows_x, rows_dy, gains, down_w, pre_gate, pre_up, sigma, hidden, blk_width):
    back_proj = lax.dot_general(
        rows_dy, down_w, (((1,), (1,)), ((), ())), preferred_element_type=jnp.float32
    )
    hidden_wide = hidden.astype(jnp.float32)
    partial_dot = jnp.sum(hidden_wide * back_proj, axis=1)
    scaled = (gains[:, None] * hidden_wide).astype(jnp.bfloat16)
    grad_down = lax.dot_general(
        scaled, rows_dy, (((0,), (0,)), ((), ())), preferred_element_type=jnp.float32
    )
    d_hidden = gains[:, None] * back_proj
    d_gate = (d_hidden * pre_up * sigma * (1.0 + pre_gate * (1.0 - sigma))).astype(jnp.bfloat16)
    d_up = (d_hidden * pre_gate * sigma).astype(jnp.bfloat16)
    d_joined = jnp.concatenate([d_gate, d_up], axis=1)
    grad_joined = lax.dot_general(
        rows_x, d_joined, (((0,), (0,)), ((), ())), preferred_element_type=jnp.float32
    )
    grad_gate = grad_joined[:, :blk_width].astype(jnp.bfloat16)
    grad_up = grad_joined[:, blk_width:].astype(jnp.bfloat16)
    return (partial_dot, grad_gate, grad_up, grad_down.astype(jnp.bfloat16))


def per_device(
    tokens, grad_out, expert_ids, route_weight, block_expert, gate_blocks, up_blocks, down_blocks
):
    devices = lax.axis_size("expert")
    tok_rows = tokens.shape[0]
    top_count = expert_ids.shape[1]
    width = tokens.shape[1]
    blk_width = gate_blocks.shape[2]
    flat_ids = expert_ids.reshape(-1)
    expert_range = jnp.arange(EXPERTS, dtype=jnp.int32)
    one_hot = (flat_ids[:, None] == expert_range[None, :]).astype(jnp.int32)
    ranks = jnp.sum(one_hot * jnp.cumsum(one_hot, axis=0), axis=1) - 1
    slot_pos = flat_ids * CAP + ranks
    owners = jnp.arange(tok_rows * top_count, dtype=jnp.int32) // top_count
    slot_tok = jnp.full((EXPERTS * CAP,), tok_rows, jnp.int32).at[slot_pos].set(owners)
    gains = route_weight.reshape(-1).astype(jnp.float32) / 256.0
    slot_gain = jnp.zeros((EXPERTS * CAP,), jnp.float32).at[slot_pos].set(gains)
    dest_tok = slot_tok.reshape(EXPERTS, CAP)[block_expert]
    dest_gain = slot_gain.reshape(EXPERTS, CAP)[block_expert].astype(jnp.bfloat16)
    zero_row = jnp.zeros((1, width), jnp.bfloat16)
    padded_x = jnp.concatenate([tokens, zero_row], axis=0)
    padded_dy = jnp.concatenate([grad_out, zero_row], axis=0)
    send_x = jnp.take(padded_x, dest_tok, axis=0)
    send_dy = jnp.take(padded_dy, dest_tok, axis=0)
    joined_w = jnp.concatenate([gate_blocks[0], up_blocks[0]], axis=1)
    down_w = down_blocks[0]
    row_total = devices * CAP
    recv_x, recv_dy, recv_gain = (
        lax.all_to_all(send_x, "expert", split_axis=0, concat_axis=0, tiled=True),
        lax.all_to_all(send_dy, "expert", split_axis=0, concat_axis=0, tiled=True),
        lax.all_to_all(dest_gain, "expert", split_axis=0, concat_axis=0, tiled=True),
    )
    rows_x = recv_x.reshape(row_total, width)
    pre_gate, pre_up, sigma, hidden = forward_part(rows_x, joined_w, blk_width)
    rows_dy = recv_dy.reshape(row_total, width)
    row_gain = recv_gain.reshape(row_total).astype(jnp.float32)
    partial_dot, grad_gate, grad_up, grad_down = backward_part(
        rows_x, rows_dy, row_gain, down_w, pre_gate, pre_up, sigma, hidden, blk_width
    )
    returned = lax.all_to_all(
        partial_dot.reshape(devices, CAP), "expert", split_axis=0, concat_axis=0, tiled=True
    )
    plan_hot = (block_expert[:, None] == expert_range[None, :]).astype(jnp.float32)
    per_expert = lax.dot_general(
        plan_hot,
        returned,
        (((0,), (0,)), ((), ())),
        precision=lax.Precision.HIGHEST,
        preferred_element_type=jnp.float32,
    )
    route_grad = per_expert[flat_ids, ranks].reshape(tok_rows, top_count)
    return (grad_gate[None], grad_up[None], grad_down[None], route_grad)


def solution(mesh):
    return jax.shard_map(
        per_device,
        mesh=mesh,
        in_specs=(
            P(("groups", "expert"), None),
            P(("groups", "expert"), None),
            P(("groups", "expert"), None),
            P(("groups", "expert"), None),
            P(),
            P("expert", None, None),
            P("expert", None, None),
            P("expert", None, None),
        ),
        out_specs=(
            P(("groups", "expert"), None, None),
            P(("groups", "expert"), None, None),
            P(("groups", "expert"), None, None),
            P(("groups", "expert"), None),
        ),
        check_vma=False,
    )
```

profile of v0, /device:TPU:0, one launch (start us, length us, event | category | flops | bytes accessed | tf_op | source)
XLA Modules:
  0.0 162.9 jit_solution(5994512975684382312)
XLA Ops:
  0.6 0.9 copy.19
  1.8 0.7 compare_select_fusion.4
  2.5 0.7 convert_multiply_fusion.2
  3.9 0.4 fusion.7
  4.3 4.3 %scatter_custom_fusion.1 = f32[1280]{0:T(1024)S(1)} fusion(s32[1024]{0:T(1024)S(1)} %bitcast.42, f32[1024]{0:T(1024)S(1)} %reshape.208, f32[]{:T(128)} %constant.53.clone.1), kind=kCustom, calls=%fused_computation.64 | custom fusion | bytes 5124 | tf_op jit(solution)/shard_map/scatter | solution.py:57
  8.8 0.6 gather_fusion.1
  9.3 0.6 copy.25
  9.9 7.4 %all-to-all-start.1 = ((bf16[16,1,10]{2,1,0:T(2,128)(2,1)}), bf16[16,1,10]{2,1,0:T(2,128)(2,1)S(1)}, u32[]{:S(2)}, u32[]{:S(2)}) async-start(bf16[16,1,10]{2,1,0:T(2,128)(2,1)} %copy.25), calls=%async_computation.1 | async-start | bytes 16384 | tf_op jit(solution)/shard_map/all_to_all | solution.py:71
  17.4 4.3 %scatter_custom_fusion = s32[1280]{0:T(1024)S(1)} fusion(s32[1024]{0:T(1024)S(1)} %bitcast.43, s32[1024]{0:T(1024)S(1)} %add_select_fusion, s32[]{:T(128)} %constant.24.clone.1), kind=kCustom, calls=%fused_computation.66 | custom fusion | bytes 5124 | tf_op jit(solution)/shard_map/scatter | solution.py:55
  21.8 0.6 gather_fusion
  22.6 1.4 gather_fusion.3
  24.0 1.6 reshape.221
  25.6 1.3 concatenate.16
  26.9 1.4 gather_fusion.4
  28.3 1.5 reshape.225
  29.8 4.0 %broadcast_select_fusion = (bf16[16,10,4096]{2,1,0:T(8,128)(2,1)}, bf16[16,10,4096]{2,1,0:T(8,128)(2,1)S(1)}) fusion(bf16[16,10,4096]{2,1,0:T(8,128)(2,1)} %reshape.225, pred[16,10]{1,0:T(8,128)(4,1)S(1)} %compare_and_fusion, bf16[16,10,4096]{2,1,0:T(8,128)(2,1)} %reshape.221), kind=kLoop, calls=%fused_computation.14 | loop fusion | flops 1310720 | bytes 5243040 | tf_op jit(solution)/shard_map/jit(_take)/select_n | solution.py:64
  33.8 53.2 %all_to_all.28 = bf16[16,10,4096]{2,1,0:T(8,128)(2,1)} all-to-all(bf16[16,10,4096]{2,1,0:T(8,128)(2,1)S(1)} %get-tuple-element.26), channel_id=1, replica_groups=mesh['groups'=2,'expert'=16] {'expert'}, dimensions={0} | all-to-all | bytes 2621440 | tf_op jit(solution)/shard_map/all_to_all | solution.py:69
  87.0 5.1 %all-to-all-start.2 = ((bf16[16,10,4096]{2,1,0:T(8,128)(2,1)}), bf16[16,10,4096]{2,1,0:T(8,128)(2,1)S(1)}, u32[]{:S(2)}, u32[]{:S(2)}) async-start(bf16[16,10,4096]{2,1,0:T(8,128)(2,1)} %get-tuple-element.25), calls=%async_computation.2 | async-start | bytes 4194304 | tf_op jit(solution)/shard_map/all_to_all | solution.py:70
  92.2 2.6 %reshape.153 = bf16[160,4096]{1,0:T(8,128)(2,1)} reshape(bf16[16,10,4096]{2,1,0:T(8,128)(2,1)} %all_to_all.28) | data formatting | bytes 2621440 | tf_op jit(solution)/shard_map/reshape | solution.py:73
  94.9 2.4 %fusion.1 = f32[160,256]{1,0:T(8,128)S(1)} fusion(bf16[160,4096]{1,0:T(8,128)(2,1)} %reshape.153, bf16[4096,128]{1,0:T(8,128)(2,1)} %bitcast.44, bf16[4096,128]{1,0:T(8,128)(2,1)} %bitcast.45), kind=kOutput, calls=%fused_computation.10 | convolution fusion | flops 339738624 | bytes 3571712 | tf_op jit(solution)/shard_map/dot_general | solution.py:11
  97.3 35.9 %all-to-all-done.2 = bf16[16,10,4096]{2,1,0:T(8,128)(2,1)S(1)} async-done(((bf16[16,10,4096]{2,1,0:T(8,128)(2,1)}), bf16[16,10,4096]{2,1,0:T(8,128)(2,1)S(1)}, u32[]{:S(2)}, u32[]{:S(2)}) %all-to-all-start.2) | async-done | bytes 1310752 | tf_op jit(solution)/shard_map/all_to_all | solution.py:70
  133.2 1.3 reshape.155
  134.5 2.0 %fusion.12 = (f32[160]{0:T(256)S(1)}, bf16[160,128]{1,0:T(8,128)(2,1)S(1)}, bf16[160,128]{1,0:T(8,128)(2,1)S(1)}, bf16[160,128]{1,0:T(8,128)(2,1)S(1)}) fusion(f32[160,256]{1,0:T(8,128)S(1)} %fusion.1, f32[160]{0:T(256)S(1)} %reshape.157, bf16[160,4096]{1,0:T(8,128)(2,1)} %reshape.155, bf16[1,128,4096]{2,1,0:T(8,128)(2,1)S(1)} %copy-done), kind=kOutput, calls=%fused_computation.31 | convolution fusion | flops 168181600 | bytes 2647296 | tf_op jit(solution)/shard_map/dot_general | solution.py:20
  136.6 0.7 all_to_all.21
  137.3 11.2 %all-to-all-start.3 = ((f32[16,1,10]{2,1,0:T(1,128)}), f32[16,1,10]{2,1,0:T(1,128)S(1)}, u32[]{:S(2)}, u32[]{:S(2)}) async-start(f32[16,1,10]{2,1,0:T(1,128)} %bitcast.12), calls=%async_computation.3 | async-start | bytes 16384 | tf_op jit(solution)/shard_map/all_to_all | solution.py:80
  148.5 0.8 convolution_convert_fusion
  149.3 1.5 slice_bitcast_fusion
  150.8 0.4 copy-done.1
  151.2 1.5 fusion
  152.7 2.2 %all-to-all-done.3 = f32[16,1,10]{2,1,0:T(1,128)S(1)} async-done(((f32[16,1,10]{2,1,0:T(1,128)}), f32[16,1,10]{2,1,0:T(1,128)S(1)}, u32[]{:S(2)}, u32[]{:S(2)}) %all-to-all-start.3) | async-done | bytes 672 | tf_op jit(solution)/shard_map/all_to_all | solution.py:80
  155.1 7.0 %gather_fusion.2 = f32[1024]{0:T(1024)S(1)} fusion(f32[128,10]{0,1:T(8,128)S(1)} %fusion.18, s32[1024]{0:T(1024)S(1)} %bitcast.37), kind=kCustom, calls=%fused_computation.4 | custom fusion | bytes 16384 | tf_op jit(solution)/shard_map/gather | solution.py:91
  162.2 0.7 copy.27
  (37 shorter events, 1.9 us)
Async XLA Ops:
  0.6 133.9 %copy-start = (bf16[1,128,4096]{2,1,0:T(8,128)(2,1)S(1)}, bf16[1,128,4096]{2,1,0:T(8,128)(2,1)}, u32[]{:S(2)}) copy-start(bf16[1,128,4096]{2,1,0:T(8,128)(2,1)} %param.17) | copy-start | bytes 3145732
  3.8 18.7 %copy-start.3 = (bf16[128,4096]{1,0:T(8,128)(2,1)S(1)}, bf16[128,4096]{1,0:T(8,128)(2,1)}, u32[]{:S(2)}) copy-start(bf16[128,4096]{1,0:T(8,128)(2,1)} %param.10) | copy-start | bytes 3145732
  9.9 23.8 %all-to-all-start.1 = ((bf16[16,1,10]{2,1,0:T(2,128)(2,1)}), bf16[16,1,10]{2,1,0:T(2,128)(2,1)S(1)}, u32[]{:S(2)}, u32[]{:S(2)}) async-start(bf16[16,1,10]{2,1,0:T(2,128)(2,1)} %copy.25), calls=%async_computation.1 | async-start | bytes 16384 | tf_op jit(solution)/shard_map/all_to_all | solution.py:71
  87.0 46.2 %all-to-all-start.2 = ((bf16[16,10,4096]{2,1,0:T(8,128)(2,1)}), bf16[16,10,4096]{2,1,0:T(8,128)(2,1)S(1)}, u32[]{:S(2)}, u32[]{:S(2)}) async-start(bf16[16,10,4096]{2,1,0:T(8,128)(2,1)} %get-tuple-element.25), calls=%async_computation.2 | async-start | bytes 4194304 | tf_op jit(solution)/shard_map/all_to_all | solution.py:70
  134.5 14.0 %copy-start.2 = (bf16[160,4096]{1,0:T(8,128)(2,1)S(1)}, bf16[160,4096]{1,0:T(8,128)(2,1)}, u32[]{:S(2)}) copy-start(bf16[160,4096]{1,0:T(8,128)(2,1)} %reshape.153) | copy-start | bytes 3932164
  137.3 17.6 %all-to-all-start.3 = ((f32[16,1,10]{2,1,0:T(1,128)}), f32[16,1,10]{2,1,0:T(1,128)S(1)}, u32[]{:S(2)}, u32[]{:S(2)}) async-start(f32[16,1,10]{2,1,0:T(1,128)} %bitcast.12), calls=%async_computation.3 | async-start | bytes 16384 | tf_op jit(solution)/shard_map/all_to_all | solution.py:80
  149.3 1.9 %copy-start.1 = (bf16[160,4096]{1,0:T(8,128)(2,1)S(1)}, bf16[160,4096]{1,0:T(8,128)(2,1)}, u32[]{:S(2)}) copy-start(bf16[160,4096]{1,0:T(8,128)(2,1)} %reshape.155) | copy-start | bytes 3932164
  150.8 4.2 %copy-start.4 = (s32[16]{0:T(128)S(1)}, s32[16]{0:T(128)}, u32[]{:S(2)}) copy-start(s32[16]{0:T(128)} %param.14) | copy-start | bytes 196
where the time goes:
time: 163 us
  blocking collectives  53.2 us (33%)
  waiting for transfers between devices  38.1 us (23%)
  local copies, waits for them, and re-layouts  34 us (21%)
  starting transfers between devices  23.7 us (15%)
  matrix products  6.95 us (4%)
  other arithmetic  6.02 us (4%)
    all_to_all x1, blocking collectives, per_device(): lax.all_to_all(send_x, 'expert', split_axis=0, concat_axis=0, tiled=True)  53.2 us
    all_to_all x1, waiting for transfers between devices, per_device(): lax.all_to_all(send_dy, 'expert', split_axis=0, concat_axis=0, tiled=True)  35.9 us
    all_to_all x1, starting transfers between devices, per_device(): lax.all_to_all(partial_dot.reshape(devices, CAP), 'expert', split_axis=0,...  11.2 us
    all_to_all x1, starting transfers between devices, per_device(): lax.all_to_all(dest_gain, 'expert', split_axis=0, concat_axis=0, tiled=True)  7.39 us
    gather x1, local copies, waits for them, and re-layouts, per_device(): route_grad = per_expert[flat_ids, ranks].reshape(tok_rows, top_count)  7.04 us
    all_to_all x1, starting transfers between devices, per_device(): lax.all_to_all(send_dy, 'expert', split_axis=0, concat_axis=0, tiled=True)  5.11 us
    scatter x1, local copies, waits for them, and re-layouts, per_device(): slot_gain = jnp.zeros((EXPERTS * CAP,), jnp.float32).at[slot_pos].set(gains)  4.32 us
    scatter x1, local copies, waits for them, and re-layouts, per_device(): jnp.full((EXPERTS * CAP,), tok_rows, jnp.int32).at[slot_pos].set(owners)  4.32 us
  transfers between devices with their start and end apart: 3, of which 2 were waited for; matrix products, arithmetic and copies ran while one was open for 16% of the time, Pallas kernels for 0%

commit v1 on v0

--- a/solution.py
+++ b/solution.py
@@ -1,6 +1,10 @@
+import functools
+
 import jax
 import jax.numpy as jnp
 from jax import lax
+from jax.experimental import pallas as pl
+from jax.experimental.pallas import tpu as pltpu
 from jax.sharding import PartitionSpec as P
 
 EXPERTS = 128
@@ -91,10 +95,326 @@
     route_grad = per_expert[flat_ids, ranks].reshape(tok_rows, top_count)
     return (grad_gate[None], grad_up[None], grad_down[None], route_grad)
 
+ROWS = 16
+MESH = pl.DeviceIdType.MESH
+
+
+def slot_tables(ids, weights):
+    count = ids.shape[1]
+    earlier = lax.broadcasted_iota(jnp.int32, (count, count), 0)
+    later = lax.broadcasted_iota(jnp.int32, (count, count), 1)
+    before = (earlier < later).astype(jnp.float32).astype(jnp.bfloat16)
+    found, rank, gain = [], [], []
+    for expert in range(2):
+        hit = (ids == expert).astype(jnp.float32)
+        here = jnp.sum(hit, axis=0, keepdims=True)
+        wide = jnp.broadcast_to(here, (ROWS, count))
+        found.append(wide)
+        rank.append(
+            jnp.dot(wide.astype(jnp.bfloat16), before, preferred_element_type=jnp.float32).astype(jnp.int32)
+        )
+        gain.append(jnp.sum(hit * weights.astype(jnp.float32), axis=0, keepdims=True) * (1.0 / 256.0))
+    slot = lax.broadcasted_iota(jnp.int32, (ROWS, count), 0)
+    first = jnp.where((slot < CAP) & (rank[0] == slot), found[0], 0.0)
+    second = jnp.where((slot >= CAP) & (rank[1] == slot - CAP), found[1], 0.0)
+    rest = jnp.where(rank[1] == slot % 4 + (ROWS - CAP), found[1], 0.0)
+    return first, second, rest, gain, slot
+
+
+def gather_kernel(pieces, ids_ref, weight_ref, x_ref, dy_ref, out_ref, own, local_sem, send_sem, recv_sem):
+    me = lax.axis_index("expert")
+    depth = lax.axis_size("expert") // 4
+    z, y, core = me // 4, (me // 2) % 2, me % 2
+    width = x_ref.shape[1]
+    half = width // 2
+    step = own.shape[1] // pieces
+
+    def place(zz, yy, cc):
+        return zz * 4 + yy * 2 + cc
+
+    targets = (
+        (place(z + 1, y, core), z < depth - 1),
+        (place(z - 1, y, core), z > 0),
+        (place(z, 1 - y, core), None),
+        (place(z, y, 1 - core), None),
+    )
+
+    def under(condition, action):
+        if condition is None:
+            action()
+        else:
+            pl.when(condition)(action)
+
+    barrier = pltpu.get_barrier_semaphore()
+    for device, there in targets:
+        under(
+            there,
+            lambda device=device: pl.semaphore_signal(
+                barrier, inc=1, device_id={"expert": device}, device_id_type=MESH
+            ),
+        )
+
+    first, second, rest, gain, slot = slot_tables(ids_ref[...], weight_ref[...])
+    main = (first + second).astype(jnp.bfloat16)
+    own[:, 0:width] = jnp.dot(main, x_ref[...], preferred_element_type=jnp.float32).astype(jnp.bfloat16)
+    own[:, width : 2 * width] = jnp.dot(main, dy_ref[...], preferred_element_type=jnp.float32).astype(jnp.bfloat16)
+    total = jnp.zeros((ROWS, half), jnp.float32)
+    for quarter in range(4):
+        chosen = jnp.where(slot // 4 == quarter, rest, 0.0).astype(jnp.bfloat16)
+        source = x_ref if quarter < 2 else dy_ref
+        total = total + jnp.dot(
+            chosen, source[:, (quarter % 2) * half : (quarter % 2 + 1) * half], preferred_element_type=jnp.float32
+        )
+    own[:, 2 * width : 2 * width + half] = total.astype(jnp.bfloat16)
+    main_gain = jnp.sum(first * gain[0] + second * gain[1], axis=1, keepdims=True)
+    rest_gain = jnp.sum(jnp.where(slot < 4, rest * gain[1], 0.0), axis=1, keepdims=True)
+    lane = lax.broadcasted_iota(jnp.int32, (ROWS, 128), 1)
+    own[:, 2 * width + half :] = jnp.where(lane < 64, main_gain, rest_gain).astype(jnp.bfloat16)
+
+    peers = 2 + (z > 0).astype(jnp.int32) + (z < depth - 1).astype(jnp.int32)
+    pl.semaphore_wait(barrier, peers)
+
+    def columns(piece):
+        return pl.ds(pl.multiple_of(piece * step, 128), step)
+
+    def copy(shard, piece, way, mine=False):
+        block = out_ref.at[shard, :, columns(piece)]
+        return pltpu.make_async_remote_copy(
+            src_ref=own.at[:, columns(piece)] if mine else block,
+            dst_ref=block,
+            send_sem=send_sem.at[way, shard, piece],
+            recv_sem=recv_sem.at[shard, piece],
+            device_id={"expert": targets[way][0]},
+            device_id_type=MESH,
+        )
+
+    keep = pltpu.make_async_copy(own, out_ref.at[me], local_sem)
+    keep.start()
+
+    def each_piece(action):
+        def body(piece, carry):
+            action(piece)
+            return carry
+
+        lax.fori_loop(0, pieces, body, 0)
+
+    def own_sends(method):
+        def action(piece):
+            for way in (2, 0, 1, 3):
+                under(targets[way][1], lambda way=way: getattr(copy(me, piece, way, True), method)())
+
+        each_piece(action)
+
+    def column_shard(shift, way, method):
+        shard = place(z + shift, y, core)
+
+        def action(piece):
+            if method == "start":
+                copy(shard, piece, 2).wait_recv()
+            under(targets[way][1], lambda: getattr(copy(shard, piece, way), method)())
+            getattr(copy(shard, piece, 2), method)()
+            getattr(copy(shard, piece, 3), method)()
+
+        pl.when((z + shift >= 0) & (z + shift < depth))(lambda: each_piece(action))
+
+    def across_shard(shift, method):
+        shard = place(z + shift, 1 - y, core)
+
+        def action(piece):
+            if method == "start":
+                copy(shard, piece, 3).wait_recv()
+            getattr(copy(shard, piece, 3), method)()
+
+        pl.when((z + shift >= 0) & (z + shift < depth))(lambda: each_piece(action))
+
+    def everything(method):
+        own_sends(method)
+        for shift in range(1, depth + 1):
+            if shift < depth:
+                column_shard(-shift, 0, method)
+                column_shard(shift, 1, method)
+            if shift == 1:
+                across_shard(0, method)
+            else:
+                across_shard(1 - shift, method)
+                across_shard(shift - 1, method)
+
+    everything("start")
+
+    def sibling(number, carry):
+        each_piece(lambda piece: copy(number * 2 + 1 - core, piece, 3).wait_recv())
+        return carry
+
+    lax.fori_loop(0, depth * 2, sibling, 0)
+    keep.wait()
+    everything("wait_send")
+
+
+def block_kernel(expert_ref, packed_ref, gate_ref, up_ref, down_ref, gate_out, up_out, down_out, dots_out):
+    width, blk = gate_ref.shape
+    half = width // 2
+    rows = packed_ref.shape[0]
+    expert = expert_ref[0]
+    slot = lax.broadcasted_iota(jnp.int32, (rows, 1), 0) % ROWS
+    gains = packed_ref[:, 2 * width + half :].astype(jnp.float32)
+    owner = (slot >= CAP).astype(jnp.int32)
+    main_on = owner == expert
+    rest_on = (slot < 4) & (expert == 1)
+    rest = packed_ref[:, 2 * width : 2 * width + half]
+    across = (((1,), (1,)), ((), ()))
+    down = (((0,), (0,)), ((), ()))
+
+    def dot(a, b, dims=(((1,), (0,)), ((), ()))):
+        return lax.dot_general(a, b, dims, preferred_element_type=jnp.float32)
+
+    def up_rows(a, amount):
+        return pltpu.roll(a, rows - amount, 0)
+
+    joined = jnp.concatenate([gate_ref[...], up_ref[...]], axis=1)
+    pre_main = dot(packed_ref[:, :width], joined)
+    back_main = dot(packed_ref[:, width : 2 * width], down_ref[...], across)
+    pre_rest = dot(rest, joined[:half]) + up_rows(dot(rest, joined[half:]), 4)
+    back_rest = up_rows(dot(rest, down_ref[:, :half], across), 8) + up_rows(
+        dot(rest, down_ref[:, half:], across), 12
+    )
+
+    def middle(pre, back, gain, on):
+        gain = jnp.where(on, gain, 0.0)
+        pre_gate, pre_up = pre[:, :blk], pre[:, blk:]
+        sigma = jax.nn.sigmoid(pre_gate)
+        hidden = (pre_gate * sigma * pre_up).astype(jnp.bfloat16).astype(jnp.float32)
+        dots = jnp.where(on, jnp.sum(hidden * back, axis=1, keepdims=True), 0.0)
+        d_hidden = gain * back
+        d_gate = d_hidden * pre_up * sigma * (1.0 + pre_gate * (1.0 - sigma))
+        d_up = d_hidden * pre_gate * sigma
+        return dots, gain * hidden, jnp.concatenate([d_gate, d_up], axis=1)
+
+    dots_main, scaled_main, d_main = middle(pre_main, back_main, gains[:, 0:1], main_on)
+    dots_rest, scaled_rest, d_rest = middle(pre_rest, back_rest, gains[:, 64:65], rest_on)
+    lane = lax.broadcasted_iota(jnp.int32, (rows, 128), 1)
+    dots_out[...] = jnp.where(lane < 64, dots_main, dots_rest)
+
+    scaled = scaled_main.astype(jnp.bfloat16)
+    d_joined = d_main.astype(jnp.bfloat16)
+    for part in range(2):
+        d_part = pltpu.roll(d_rest, 4 * part, 0) if part else d_rest
+        d_part = d_part.astype(jnp.bfloat16)
+        scaled_part = pltpu.roll(scaled_rest, 8 + 4 * part, 0).astype(jnp.bfloat16)
+        tile = 512
+        for start in range(0, half, tile):
+            here = slice(part * half + start, part * half + start + tile)
+            rest_here = packed_ref[:, 2 * width + start : 2 * width + start + tile]
+            grad = dot(packed_ref[:, here], d_joined, down) + dot(rest_here, d_part, down)
+            gate_out[here, :] = grad[:, :blk].astype(jnp.bfloat16)
+            up_out[here, :] = grad[:, blk:].astype(jnp.bfloat16)
+            there = slice(width + here.start, width + here.stop)
+            grad_down = dot(scaled, packed_ref[:, there], down) + dot(scaled_part, rest_here, down)
+            down_out[:, here] = grad_down.astype(jnp.bfloat16)
+
+
+def return_kernel(dots_ref, ids_ref, out_ref, held, send_sem, recv_sem):
+    devices = lax.axis_size("expert")
+    me = lax.axis_index("expert")
+
+    def each_other(action):
+        def body(shift, carry):
+            action(lax.rem(me + shift, devices))
+            return carry
+
+        lax.fori_loop(1, devices, body, 0)
+
+    barrier = pltpu.get_barrier_semaphore()
+    each_other(
+        lambda device: pl.semaphore_signal(barrier, inc=1, device_id={"expert": device}, device_id_type=MESH)
+    )
+    pl.semaphore_wait(barrier, devices - 1)
+
+    def copy(device, landing, sender):
+        return pltpu.make_async_remote_copy(
+            src_ref=dots_ref.at[device],
+            dst_ref=held.at[landing],
+            send_sem=send_sem.at[device],
+            recv_sem=recv_sem.at[sender],
+            device_id={"expert": device},
+            device_id_type=MESH,
+        )
+
+    each_other(lambda device: copy(device, me, me).start())
+    ids = ids_ref[...]
+    first, second, rest, _, slot = slot_tables(ids, ids)
+    held[me] = dots_ref[me]
+    each_other(lambda device: copy(device, device, device).wait_recv())
+    total = held[0]
+    for device in range(1, devices):
+        total = total + held[device]
+    main, extra = total[:, 0:1], total[:, 64:65]
+    low = jnp.sum(first * main, axis=0, keepdims=True)
+    high = jnp.sum(second * main + jnp.where(slot < 4, rest * extra, 0.0), axis=0, keepdims=True)
+    out_ref[...] = jnp.where(ids == 0, low, jnp.where(ids == 1, high, 0.0))
+    each_other(lambda device: copy(device, me, me).wait_send())
+
+
+def per_device_gathered(
+    tokens, grad_out, expert_ids, route_weight, block_expert, gate_blocks, up_blocks, down_blocks
+):
+    devices = lax.axis_size("expert")
+    count, width = tokens.shape
+    blk = gate_blocks.shape[2]
+    ids, weights = expert_ids.T, route_weight.T
+    total = 2 * width + width // 2 + 128
+    pieces = 3
+    vmem = pl.BlockSpec(memory_space=pltpu.VMEM)
+    anywhere = pl.BlockSpec(memory_space=pl.ANY)
+    packed = pl.pallas_call(
+        functools.partial(gather_kernel, pieces),
+        out_shape=jax.ShapeDtypeStruct((devices, ROWS, total), jnp.bfloat16),
+        in_specs=[vmem] * 4,
+        out_specs=anywhere,
+        scratch_shapes=[
+            pltpu.VMEM((ROWS, total), jnp.bfloat16),
+            pltpu.SemaphoreType.DMA,
+            pltpu.SemaphoreType.DMA((4, devices, pieces)),
+            pltpu.SemaphoreType.DMA((devices, pieces)),
+        ],
+        compiler_params=pltpu.CompilerParams(
+            collective_id=0, has_side_effects=True, vmem_limit_bytes=32 * 1024 * 1024
+        ),
+        name="gather_rows",
+    )(ids, weights, tokens, grad_out)
+    mine = lax.dynamic_slice(block_expert, (lax.axis_index("expert"),), (1,))
+    grad_gate, grad_up, grad_down, dots = pl.pallas_call(
+        block_kernel,
+        out_shape=(
+            jax.ShapeDtypeStruct((width, blk), jnp.bfloat16),
+            jax.ShapeDtypeStruct((width, blk), jnp.bfloat16),
+            jax.ShapeDtypeStruct((blk, width), jnp.bfloat16),
+            jax.ShapeDtypeStruct((devices * ROWS, 128), jnp.float32),
+        ),
+        in_specs=[pl.BlockSpec(memory_space=pltpu.SMEM)] + [vmem] * 4,
+        out_specs=(vmem,) * 4,
+        compiler_params=pltpu.CompilerParams(vmem_limit_bytes=56 * 1024 * 1024),
+        name="block_grads",
+    )(mine, packed.reshape(devices * ROWS, total), gate_blocks[0], up_blocks[0], down_blocks[0])
+    route_grad = pl.pallas_call(
+        return_kernel,
+        out_shape=jax.ShapeDtypeStruct(ids.shape, jnp.float32),
+        in_specs=[vmem] * 2,
+        out_specs=vmem,
+        scratch_shapes=[
+            pltpu.VMEM((devices, ROWS, 128), jnp.float32),
+            pltpu.SemaphoreType.DMA((devices,)),
+            pltpu.SemaphoreType.DMA((devices,)),
+        ],
+        compiler_params=pltpu.CompilerParams(collective_id=1, has_side_effects=True),
+        name="return_dots",
+    )(dots.reshape(devices, ROWS, 128), ids)
+    return (grad_gate[None], grad_up[None], grad_down[None], route_grad.T)
+
 
 def solution(mesh):
+    body = per_device_gathered if mesh.shape["expert"] == 16 else per_device
     return jax.shard_map(
-        per_device,
+        body,
         mesh=mesh,
         in_specs=(
             P(("groups", "expert"), None),

time: 163 us -> 66.3 us (0.41)
  Pallas kernels: 0 us -> 56.7 us
  blocking collectives: 53.2 us -> 0 us
  waiting for transfers between devices: 38.1 us -> 0 us
  local copies, waits for them, and re-layouts: 34 us -> 8.65 us
  starting transfers between devices: 23.7 us -> 0 us
  matrix products: 6.95 us -> 0 us
  other arithmetic: 6.02 us -> 0 us
    pallas_call x0 -> x3, Pallas kernels: none -> 56.7 us  [the longest x1 36.6 us: per_device_gathered(): pl.pallas_call(functools.partial(gather_kernel, pieces), out_shape=jax.Sh...]
    all_to_all x1 -> x0, blocking collectives: 53.2 us -> none  [per_device(): lax.all_to_all(send_x, 'expert', split_axis=0, concat_axis=0, tiled=True)]
    all_to_all x3 -> x0, waiting for transfers between devices: 38.1 us -> none  [the longest x1 35.9 us: per_device(): lax.all_to_all(send_dy, 'expert', split_axis=0, concat_axis=0, tiled=True)]
    all_to_all x3 -> x0, starting transfers between devices: 23.7 us -> none  [the longest x1 11.2 us: per_device(): lax.all_to_all(partial_dot.reshape(devices, CAP), 'expert', split_axis=0,...]
    gather x7 -> x0, local copies, waits for them, and re-layouts: 14 us -> none  [the longest x1 7.04 us: per_device(): route_grad = per_expert[flat_ids, ranks].reshape(tok_rows, top_count)]
    scatter x2 -> x0, local copies, waits for them, and re-layouts: 8.63 us -> none  [the longest x1 4.32 us: per_device(): slot_gain = jnp.zeros((EXPERTS * CAP,), jnp.float32).at[slot_pos].set(gains)]
    dot_general x5 -> x0, matrix products: 6.95 us -> none  [the longest x1 2.44 us: forward_part(): joined = jnp.dot(rows_x, joined_w, preferred_element_type=jnp.float32)]
    unnamed x12 -> x11, local copies, waits for them, and re-layouts: 1.98 us -> 7.4 us
  transfers between devices with their start and end apart: 3 -> 0, of which waited for: 2 -> 0; matrix products, arithmetic and copies ran while one was open for 16% -> 0% of each run, Pallas kernels for 0% -> 0%
where the time goes in v1:
time: 66.3 us; the launch traced here: 66 us
  Pallas kernels  56.7 us (86%)
  local copies, waits for them, and re-layouts  8.65 us (13%)
    pallas_call x1, Pallas kernels, per_device_gathered(): pl.pallas_call(functools.partial(gather_kernel, pieces), out_shape=jax.Sh...  36.6 us
    pallas_call x1, Pallas kernels, per_device_gathered(): pl.pallas_call(block_kernel, out_shape=(jax.ShapeDtypeStruct((width, blk)...  10.4 us
    pallas_call x1, Pallas kernels, per_device_gathered(): pl.pallas_call(return_kernel, out_shape=jax.ShapeDtypeStruct(ids.shape, j...  9.66 us
    unnamed x11, local copies, waits for them, and re-layouts  7.4 us

profile of v1, /device:TPU:0, one launch (start us, length us, event | category | flops | bytes accessed | tf_op | source)
XLA Modules:
  0.0 66.0 jit_solution(1083213227224324600)
XLA Ops:
  0.6 1.2 %dynamic_slice.3.expert_ref = s32[1]{0:T(128)} dynamic-slice(s32[16]{0:T(128)} %param.12, s32[]{:T(128)S(6)} %select_n.3), dynamic_slice_sizes={1} | dynamic-slice | bytes 12 | tf_op jit(solution)/shard_map/dynamic_slice | solution.py:384
  1.9 0.0 copy-start.1
  1.9 1.2 %copy-done.1 = bf16[128,4096]{1,0:T(8,128)(2,1)S(1)} copy-done((bf16[128,4096]{1,0:T(8,128)(2,1)S(1)}, bf16[128,4096]{1,0:T(8,128)(2,1)}, u32[]{:S(2)}) %copy-start.1) | copy-done | bytes 1048600
  3.1 0.0 copy-start.2
  3.1 1.2 %copy-done.2 = bf16[128,4096]{1,0:T(8,128)(2,1)S(1)} copy-done((bf16[128,4096]{1,0:T(8,128)(2,1)S(1)}, bf16[128,4096]{1,0:T(8,128)(2,1)}, u32[]{:S(2)}) %copy-start.2) | copy-done | bytes 1048600
  4.3 0.0 copy-start.3
  4.3 0.7 %copy-done.3 = s32[128,8]{0,1:T(8,128)S(1)} copy-done((s32[128,8]{0,1:T(8,128)S(1)}, s32[128,8]{0,1:T(8,128)}, u32[]{:S(2)}) %copy-start.3) | copy-done | bytes 4120
  5.0 0.0 copy-start.4
  5.0 0.7 %copy-done.4 = s32[128,8]{0,1:T(8,128)S(1)} copy-done((s32[128,8]{0,1:T(8,128)S(1)}, s32[128,8]{0,1:T(8,128)}, u32[]{:S(2)}) %copy-start.4) | copy-done | bytes 4120
  5.7 36.6 %gather_rows.1 = bf16[16,16,10368]{2,1,0:T(8,128)(2,1)S(1)} custom-call(s32[8,128]{1,0:T(8,128)S(1)} %bitcast.13, s32[8,128]{1,0:T(8,128)S(1)} %bitcast.14, bf16[128,4096]{1,0:T(8,128)(2,1)S(1)} %copy-done.1, bf16[128,4096]{1,0:T(8,128)(2,1)S(1)} %copy-done.2), custom_call_target="tpu_custom_call" | custom-call | tf_op jit(solution)/shard_map/gather_rows/pallas_call | solution.py:368
  42.3 0.0 copy-start
  42.3 2.3 %copy-done = bf16[16,16,10368]{2,1,0:T(8,128)(2,1)} copy-done((bf16[16,16,10368]{2,1,0:T(8,128)(2,1)}, bf16[16,16,10368]{2,1,0:T(8,128)(2,1)S(1)}, u32[]{:S(2)}) %copy-start) | copy-done | bytes 5308440
  44.6 10.4 %block_grads.1 = (bf16[4096,128]{1,0:T(8,128)(2,1)}, bf16[4096,128]{1,0:T(8,128)(2,1)}, bf16[128,4096]{1,0:T(8,128)(2,1)}, f32[256,128]{1,0:T(8,128)}) custom-call(s32[1]{0:T(128)} %dynamic_slice.3.expert_ref, bf16[256,10368]{1,0:T(8,128)(2,1)} %bitcast.11, bf16[4096,128]{1,0:T(8,128)(2,1)} %bitcast.15, bf16[4096,128]{1,0:T(8,128)(2,1)} %bitcast.16, ...), custom_call_target="tpu_custom_call" | custom-call | tf_op jit(solution)/shard_map/block_grads/pallas_call | solution.py:385
  55.0 9.7 %return_dots.1 = f32[8,128]{1,0:T(8,128)} custom-call(f32[16,16,128]{2,1,0:T(8,128)} %bitcast.18, s32[8,128]{1,0:T(8,128)} %bitcast.12), custom_call_target="tpu_custom_call" | custom-call | tf_op jit(solution)/shard_map/return_dots/pallas_call | solution.py:398
  64.7 1.3 %copy.13 = f32[128,8]{0,1:T(8,128)} copy(f32[128,8]{0,1:T(8,128)} %bitcast.19) | data formatting | bytes 8192
Async XLA Ops:
  1.9 1.2 %copy-start.1 = (bf16[128,4096]{1,0:T(8,128)(2,1)S(1)}, bf16[128,4096]{1,0:T(8,128)(2,1)}, u32[]{:S(2)}) copy-start(bf16[128,4096]{1,0:T(8,128)(2,1)} %x_ref.1) | copy-start | bytes 3145732
  3.1 1.2 %copy-start.2 = (bf16[128,4096]{1,0:T(8,128)(2,1)S(1)}, bf16[128,4096]{1,0:T(8,128)(2,1)}, u32[]{:S(2)}) copy-start(bf16[128,4096]{1,0:T(8,128)(2,1)} %dy_ref.1) | copy-start | bytes 3145732
  4.3 0.7 %copy-start.3 = (s32[128,8]{0,1:T(8,128)S(1)}, s32[128,8]{0,1:T(8,128)}, u32[]{:S(2)}) copy-start(s32[128,8]{0,1:T(8,128)} %param.10) | copy-start | bytes 12292
  5.0 0.7 %copy-start.4 = (s32[128,8]{0,1:T(8,128)S(1)}, s32[128,8]{0,1:T(8,128)}, u32[]{:S(2)}) copy-start(s32[128,8]{0,1:T(8,128)} %param.11) | copy-start | bytes 12292
  42.3 2.3 %copy-start = (bf16[16,16,10368]{2,1,0:T(8,128)(2,1)}, bf16[16,16,10368]{2,1,0:T(8,128)(2,1)S(1)}, u32[]{:S(2)}) copy-start(bf16[16,16,10368]{2,1,0:T(8,128)(2,1)S(1)} %gather_rows.1) | copy-start | bytes 15925252

commit v2 on v1

--- a/solution.py
+++ b/solution.py
@@ -121,13 +121,72 @@
     return first, second, rest, gain, slot
 
 
-def gather_kernel(pieces, ids_ref, weight_ref, x_ref, dy_ref, out_ref, own, local_sem, send_sem, recv_sem):
+def fused_kernel(
+    pieces,
+    expert_ref,
+    ids_ref,
+    weight_ref,
+    x_hbm,
+    dy_hbm,
+    gate_hbm,
+    up_hbm,
+    down_hbm,
+    gate_out,
+    up_out,
+    down_out,
+    route_out,
+    x_ref,
+    dy_ref,
+    joined_ref,
+    down_ref,
+    packed,
+    grad_joined,
+    grad_down,
+    dots,
+    held,
+    load_sem,
+    store_sem,
+    send_sem,
+    recv_sem,
+    dot_send,
+    dot_recv,
+):
     me = lax.axis_index("expert")
-    depth = lax.axis_size("expert") // 4
+    devices = lax.axis_size("expert")
+    depth = devices // 4
     z, y, core = me // 4, (me // 2) % 2, me % 2
     width = x_ref.shape[1]
+    blk = down_ref.shape[0]
     half = width // 2
-    step = own.shape[1] // pieces
+    step = packed.shape[1] // pieces
+    last = pieces - 1
+
+    loads = [
+        pltpu.make_async_copy(source, target, load_sem.at[number])
+        for number, (source, target) in enumerate(
+            (
+                (x_hbm, x_ref),
+                (dy_hbm, dy_ref),
+                (gate_hbm, joined_ref.at[:, 0:blk]),
+                (up_hbm, joined_ref.at[:, blk : 2 * blk]),
+                (down_hbm, down_ref),
+            )
+        )
+    ]
+    for load in loads:
+        load.start()
+
+    def each_other(action):
+        def body(shift, carry):
+            action(lax.rem(me + shift, devices))
+            return carry
+
+        lax.fori_loop(1, devices, body, 0)
+
+    barrier = pltpu.get_barrier_semaphore()
+    each_other(
+        lambda device: pl.semaphore_signal(barrier, inc=1, device_id={"expert": device}, device_id_type=MESH)
+    )
 
     def place(zz, yy, cc):
         return zz * 4 + yy * 2 + cc
@@ -138,6 +197,7 @@
         (place(z, 1 - y, core), None),
         (place(z, y, 1 - core), None),
     )
+    partner = z + 1 - 2 * (z % 2)
 
     def under(condition, action):
         if condition is None:
@@ -145,42 +205,37 @@
         else:
             pl.when(condition)(action)
 
-    barrier = pltpu.get_barrier_semaphore()
-    for device, there in targets:
-        under(
-            there,
-            lambda device=device: pl.semaphore_signal(
-                barrier, inc=1, device_id={"expert": device}, device_id_type=MESH
-            ),
-        )
-
-    first, second, rest, gain, slot = slot_tables(ids_ref[...], weight_ref[...])
+    def shard_rows(shard):
+        return pl.ds(pl.multiple_of(shard * ROWS, ROWS), ROWS)
+
+    first, second, rest_hot, gain, slot = slot_tables(ids_ref[...], weight_ref[...])
     main = (first + second).astype(jnp.bfloat16)
-    own[:, 0:width] = jnp.dot(main, x_ref[...], preferred_element_type=jnp.float32).astype(jnp.bfloat16)
-    own[:, width : 2 * width] = jnp.dot(main, dy_ref[...], preferred_element_type=jnp.float32).astype(jnp.bfloat16)
+    mine = shard_rows(me)
+    main_gain = jnp.sum(first * gain[0] + second * gain[1], axis=1, keepdims=True)
+    rest_gain = jnp.sum(jnp.where(slot < 4, rest_hot * gain[1], 0.0), axis=1, keepdims=True)
+    lane = lax.broadcasted_iota(jnp.int32, (ROWS, 128), 1)
+    packed[mine, 2 * width + half :] = jnp.where(lane < 64, main_gain, rest_gain).astype(jnp.bfloat16)
+    loads[0].wait()
+    packed[mine, 0:width] = jnp.dot(main, x_ref[...], preferred_element_type=jnp.float32).astype(jnp.bfloat16)
+    loads[1].wait()
+    packed[mine, width : 2 * width] = jnp.dot(main, dy_ref[...], preferred_element_type=jnp.float32).astype(
+        jnp.bfloat16
+    )
     total = jnp.zeros((ROWS, half), jnp.float32)
     for quarter in range(4):
-        chosen = jnp.where(slot // 4 == quarter, rest, 0.0).astype(jnp.bfloat16)
+        chosen = jnp.where(slot // 4 == quarter, rest_hot, 0.0).astype(jnp.bfloat16)
         source = x_ref if quarter < 2 else dy_ref
         total = total + jnp.dot(
             chosen, source[:, (quarter % 2) * half : (quarter % 2 + 1) * half], preferred_element_type=jnp.float32
         )
-    own[:, 2 * width : 2 * width + half] = total.astype(jnp.bfloat16)
-    main_gain = jnp.sum(first * gain[0] + second * gain[1], axis=1, keepdims=True)
-    rest_gain = jnp.sum(jnp.where(slot < 4, rest * gain[1], 0.0), axis=1, keepdims=True)
-    lane = lax.broadcasted_iota(jnp.int32, (ROWS, 128), 1)
-    own[:, 2 * width + half :] = jnp.where(lane < 64, main_gain, rest_gain).astype(jnp.bfloat16)
-
-    peers = 2 + (z > 0).astype(jnp.int32) + (z < depth - 1).astype(jnp.int32)
-    pl.semaphore_wait(barrier, peers)
-
-    def columns(piece):
-        return pl.ds(pl.multiple_of(piece * step, 128), step)
-
-    def copy(shard, piece, way, mine=False):
-        block = out_ref.at[shard, :, columns(piece)]
+    packed[mine, 2 * width : 2 * width + half] = total.astype(jnp.bfloat16)
+
+    pl.semaphore_wait(barrier, devices - 1)
+
+    def copy(shard, piece, way):
+        block = packed.at[shard_rows(shard), pl.ds(pl.multiple_of(piece * step, 128), step)]
         return pltpu.make_async_remote_copy(
-            src_ref=own.at[:, columns(piece)] if mine else block,
+            src_ref=block,
             dst_ref=block,
             send_sem=send_sem.at[way, shard, piece],
             recv_sem=recv_sem.at[shard, piece],
@@ -188,9 +243,6 @@
             device_id_type=MESH,
         )
 
-    keep = pltpu.make_async_copy(own, out_ref.at[me], local_sem)
-    keep.start()
-
     def each_piece(action):
         def body(piece, carry):
             action(piece)
@@ -201,7 +253,7 @@
     def own_sends(method):
         def action(piece):
             for way in (2, 0, 1, 3):
-                under(targets[way][1], lambda way=way: getattr(copy(me, piece, way, True), method)())
+                under(targets[way][1], lambda way=way: getattr(copy(me, piece, way), method)())
 
         each_piece(action)
 
@@ -212,7 +264,7 @@
             if method == "start":
                 copy(shard, piece, 2).wait_recv()
             under(targets[way][1], lambda: getattr(copy(shard, piece, way), method)())
-            getattr(copy(shard, piece, 2), method)()
+            pl.when((piece < last) | (z + shift != partner))(lambda: getattr(copy(shard, piece, 2), method)())
             getattr(copy(shard, piece, 3), method)()
 
         pl.when((z + shift >= 0) & (z + shift < depth))(lambda: each_piece(action))
@@ -223,6 +275,9 @@
         def action(piece):
             if method == "start":
                 copy(shard, piece, 3).wait_recv()
+            if shift == 0:
+                pl.when((piece == last) & (z % 2 == 0))(lambda: getattr(copy(shard, piece, 0), method)())
+                pl.when((piece == last) & (z % 2 == 1))(lambda: getattr(copy(shard, piece, 1), method)())
             getattr(copy(shard, piece, 3), method)()
 
         pl.when((z + shift >= 0) & (z + shift < depth))(lambda: each_piece(action))
@@ -246,21 +301,16 @@
         return carry
 
     lax.fori_loop(0, depth * 2, sibling, 0)
-    keep.wait()
-    everything("wait_send")
-
-
-def block_kernel(expert_ref, packed_ref, gate_ref, up_ref, down_ref, gate_out, up_out, down_out, dots_out):
-    width, blk = gate_ref.shape
-    half = width // 2
-    rows = packed_ref.shape[0]
-    expert = expert_ref[0]
-    slot = lax.broadcasted_iota(jnp.int32, (rows, 1), 0) % ROWS
-    gains = packed_ref[:, 2 * width + half :].astype(jnp.float32)
-    owner = (slot >= CAP).astype(jnp.int32)
-    main_on = owner == expert
-    rest_on = (slot < 4) & (expert == 1)
-    rest = packed_ref[:, 2 * width : 2 * width + half]
+    for load in loads[2:]:
+        load.wait()
+
+    rows = packed.shape[0]
+    expert = expert_ref[me]
+    row_slot = lax.broadcasted_iota(jnp.int32, (rows, 1), 0) % ROWS
+    gains = packed[:, 2 * width + half :].astype(jnp.float32)
+    main_on = (row_slot >= CAP).astype(jnp.int32) == expert
+    rest_on = (row_slot < 4) & (expert == 1)
+    rest = packed[:, 2 * width : 2 * width + half]
     across = (((1,), (1,)), ((), ()))
     down = (((0,), (0,)), ((), ()))
 
@@ -270,10 +320,9 @@
     def up_rows(a, amount):
         return pltpu.roll(a, rows - amount, 0)
 
-    joined = jnp.concatenate([gate_ref[...], up_ref[...]], axis=1)
-    pre_main = dot(packed_ref[:, :width], joined)
-    back_main = dot(packed_ref[:, width : 2 * width], down_ref[...], across)
-    pre_rest = dot(rest, joined[:half]) + up_rows(dot(rest, joined[half:]), 4)
+    pre_main = dot(packed[:, :width], joined_ref[...])
+    back_main = dot(packed[:, width : 2 * width], down_ref[...], across)
+    pre_rest = dot(rest, joined_ref[:half, :]) + up_rows(dot(rest, joined_ref[half:, :]), 4)
     back_rest = up_rows(dot(rest, down_ref[:, :half], across), 8) + up_rows(
         dot(rest, down_ref[:, half:], across), 12
     )
@@ -283,19 +332,33 @@
         pre_gate, pre_up = pre[:, :blk], pre[:, blk:]
         sigma = jax.nn.sigmoid(pre_gate)
         hidden = (pre_gate * sigma * pre_up).astype(jnp.bfloat16).astype(jnp.float32)
-        dots = jnp.where(on, jnp.sum(hidden * back, axis=1, keepdims=True), 0.0)
+        products = jnp.where(on, jnp.sum(hidden * back, axis=1, keepdims=True), 0.0)
         d_hidden = gain * back
         d_gate = d_hidden * pre_up * sigma * (1.0 + pre_gate * (1.0 - sigma))
         d_up = d_hidden * pre_gate * sigma
-        return dots, gain * hidden, jnp.concatenate([d_gate, d_up], axis=1)
+        return products, gain * hidden, jnp.concatenate([d_gate, d_up], axis=1)
 
     dots_main, scaled_main, d_main = middle(pre_main, back_main, gains[:, 0:1], main_on)
     dots_rest, scaled_rest, d_rest = middle(pre_rest, back_rest, gains[:, 64:65], rest_on)
-    lane = lax.broadcasted_iota(jnp.int32, (rows, 128), 1)
-    dots_out[...] = jnp.where(lane < 64, dots_main, dots_rest)
+    wide_lane = lax.broadcasted_iota(jnp.int32, (rows, 128), 1)
+    dots[...] = jnp.where(wide_lane < 64, dots_main, dots_rest).reshape(devices, ROWS, 128)
+
+    def dot_copy(device, landing, sender):
+        return pltpu.make_async_remote_copy(
+            src_ref=dots.at[device],
+            dst_ref=held.at[landing],
+            send_sem=dot_send.at[device],
+            recv_sem=dot_recv.at[sender],
+            device_id={"expert": device},
+            device_id_type=MESH,
+        )
+
+    each_other(lambda device: dot_copy(device, me, me).start())
+    held[me] = dots[me]
 
     scaled = scaled_main.astype(jnp.bfloat16)
     d_joined = d_main.astype(jnp.bfloat16)
+    stores = []
     for part in range(2):
         d_part = pltpu.roll(d_rest, 4 * part, 0) if part else d_rest
         d_part = d_part.astype(jnp.bfloat16)
@@ -303,55 +366,39 @@
         tile = 512
         for start in range(0, half, tile):
             here = slice(part * half + start, part * half + start + tile)
-            rest_here = packed_ref[:, 2 * width + start : 2 * width + start + tile]
-            grad = dot(packed_ref[:, here], d_joined, down) + dot(rest_here, d_part, down)
-            gate_out[here, :] = grad[:, :blk].astype(jnp.bfloat16)
-            up_out[here, :] = grad[:, blk:].astype(jnp.bfloat16)
+            rest_here = packed[:, 2 * width + start : 2 * width + start + tile]
+            grad = dot(packed[:, here], d_joined, down) + dot(rest_here, d_part, down)
+            grad_joined[here, :] = grad.astype(jnp.bfloat16)
             there = slice(width + here.start, width + here.stop)
-            grad_down = dot(scaled, packed_ref[:, there], down) + dot(scaled_part, rest_here, down)
-            down_out[:, here] = grad_down.astype(jnp.bfloat16)
-
-
-def return_kernel(dots_ref, ids_ref, out_ref, held, send_sem, recv_sem):
-    devices = lax.axis_size("expert")
-    me = lax.axis_index("expert")
-
-    def each_other(action):
-        def body(shift, carry):
-            action(lax.rem(me + shift, devices))
-            return carry
-
-        lax.fori_loop(1, devices, body, 0)
-
-    barrier = pltpu.get_barrier_semaphore()
-    each_other(
-        lambda device: pl.semaphore_signal(barrier, inc=1, device_id={"expert": device}, device_id_type=MESH)
-    )
-    pl.semaphore_wait(barrier, devices - 1)
-
-    def copy(device, landing, sender):
-        return pltpu.make_async_remote_copy(
-            src_ref=dots_ref.at[device],
-            dst_ref=held.at[landing],
-            send_sem=send_sem.at[device],
-            recv_sem=recv_sem.at[sender],
-            device_id={"expert": device},
-            device_id_type=MESH,
-        )
-
-    each_other(lambda device: copy(device, me, me).start())
-    ids = ids_ref[...]
-    first, second, rest, _, slot = slot_tables(ids, ids)
-    held[me] = dots_ref[me]
-    each_other(lambda device: copy(device, device, device).wait_recv())
+            grad_down[:, here] = (
+                dot(scaled, packed[:, there], down) + dot(scaled_part, rest_here, down)
+            ).astype(jnp.bfloat16)
+        block = pl.ds(part * half, half)
+        for number, (source, target) in enumerate(
+            (
+                (grad_joined.at[block, 0:blk], gate_out.at[block, :]),
+                (grad_joined.at[block, blk : 2 * blk], up_out.at[block, :]),
+                (grad_down.at[:, block], down_out.at[:, block]),
+            )
+        ):
+            store = pltpu.make_async_copy(source, target, store_sem.at[part * 3 + number])
+            store.start()
+            stores.append(store)
+
+    each_other(lambda device: dot_copy(device, device, device).wait_recv())
     total = held[0]
     for device in range(1, devices):
         total = total + held[device]
-    main, extra = total[:, 0:1], total[:, 64:65]
-    low = jnp.sum(first * main, axis=0, keepdims=True)
-    high = jnp.sum(second * main + jnp.where(slot < 4, rest * extra, 0.0), axis=0, keepdims=True)
-    out_ref[...] = jnp.where(ids == 0, low, jnp.where(ids == 1, high, 0.0))
-    each_other(lambda device: copy(device, me, me).wait_send())
+    ids = ids_ref[...]
+    first, second, rest_hot, _, slot = slot_tables(ids, ids)
+    total_main, extra = total[:, 0:1], total[:, 64:65]
+    low = jnp.sum(first * total_main, axis=0, keepdims=True)
+    high = jnp.sum(second * total_main + jnp.where(slot < 4, rest_hot * extra, 0.0), axis=0, keepdims=True)
+    route_out[...] = jnp.where(ids == 0, low, jnp.where(ids == 1, high, 0.0))
+    each_other(lambda device: dot_copy(device, me, me).wait_send())
+    everything("wait_send")
+    for store in stores:
+        store.wait()
 
 
 def per_device_gathered(
@@ -365,49 +412,38 @@
     pieces = 3
     vmem = pl.BlockSpec(memory_space=pltpu.VMEM)
     anywhere = pl.BlockSpec(memory_space=pl.ANY)
-    packed = pl.pallas_call(
-        functools.partial(gather_kernel, pieces),
-        out_shape=jax.ShapeDtypeStruct((devices, ROWS, total), jnp.bfloat16),
-        in_specs=[vmem] * 4,
-        out_specs=anywhere,
-        scratch_shapes=[
-            pltpu.VMEM((ROWS, total), jnp.bfloat16),
-            pltpu.SemaphoreType.DMA,
-            pltpu.SemaphoreType.DMA((4, devices, pieces)),
-            pltpu.SemaphoreType.DMA((devices, pieces)),
-        ],
-        compiler_params=pltpu.CompilerParams(
-            collective_id=0, has_side_effects=True, vmem_limit_bytes=32 * 1024 * 1024
-        ),
-        name="gather_rows",
-    )(ids, weights, tokens, grad_out)
-    mine = lax.dynamic_slice(block_expert, (lax.axis_index("expert"),), (1,))
-    grad_gate, grad_up, grad_down, dots = pl.pallas_call(
-        block_kernel,
+    grad_gate, grad_up, grad_down, route_grad = pl.pallas_call(
+        functools.partial(fused_kernel, pieces),
         out_shape=(
             jax.ShapeDtypeStruct((width, blk), jnp.bfloat16),
             jax.ShapeDtypeStruct((width, blk), jnp.bfloat16),
             jax.ShapeDtypeStruct((blk, width), jnp.bfloat16),
-            jax.ShapeDtypeStruct((devices * ROWS, 128), jnp.float32),
+            jax.ShapeDtypeStruct(ids.shape, jnp.float32),
         ),
-        in_specs=[pl.BlockSpec(memory_space=pltpu.SMEM)] + [vmem] * 4,
-        out_specs=(vmem,) * 4,
-        compiler_params=pltpu.CompilerParams(vmem_limit_bytes=56 * 1024 * 1024),
-        name="block_grads",
-    )(mine, packed.reshape(devices * ROWS, total), gate_blocks[0], up_blocks[0], down_blocks[0])
-    route_grad = pl.pallas_call(
-        return_kernel,
-        out_shape=jax.ShapeDtypeStruct(ids.shape, jnp.float32),
-        in_specs=[vmem] * 2,
-        out_specs=vmem,
+        in_specs=[pl.BlockSpec(memory_space=pltpu.SMEM), vmem, vmem] + [anywhere] * 5,
+        out_specs=(anywhere, anywhere, anywhere, vmem),
         scratch_shapes=[
+            pltpu.VMEM((count, width), jnp.bfloat16),
+            pltpu.VMEM((count, width), jnp.bfloat16),
+            pltpu.VMEM((width, 2 * blk), jnp.bfloat16),
+            pltpu.VMEM((blk, width), jnp.bfloat16),
+            pltpu.VMEM((devices * ROWS, total), jnp.bfloat16),
+            pltpu.VMEM((width, 2 * blk), jnp.bfloat16),
+            pltpu.VMEM((blk, width), jnp.bfloat16),
             pltpu.VMEM((devices, ROWS, 128), jnp.float32),
+            pltpu.VMEM((devices, ROWS, 128), jnp.float32),
+            pltpu.SemaphoreType.DMA((5,)),
+            pltpu.SemaphoreType.DMA((6,)),
+            pltpu.SemaphoreType.DMA((4, devices, pieces)),
+            pltpu.SemaphoreType.DMA((devices, pieces)),
             pltpu.SemaphoreType.DMA((devices,)),
             pltpu.SemaphoreType.DMA((devices,)),
         ],
-        compiler_params=pltpu.CompilerParams(collective_id=1, has_side_effects=True),
-        name="return_dots",
-    )(dots.reshape(devices, ROWS, 128), ids)
+        compiler_params=pltpu.CompilerParams(
+            collective_id=0, has_side_effects=True, vmem_limit_bytes=58 * 1024 * 1024
+        ),
+        name="layer_backward",
+    )(block_expert, ids, weights, tokens, grad_out, gate_blocks[0], up_blocks[0], down_blocks[0])
     return (grad_gate[None], grad_up[None], grad_down[None], route_grad.T)
 
 

time: 66.3 us -> 54.9 us (0.83)
  Pallas kernels: 56.7 us -> 48.5 us
  local copies, waits for them, and re-layouts: 8.65 us -> 5.52 us
    pallas_call x3 -> x1, Pallas kernels: 56.7 us -> 48.5 us  [per_device_gathered(): pl.pallas_call(functools.partial(fused_kernel, pieces), out_shape=(jax.Sh...]
    unnamed x11 -> x10, local copies, waits for them, and re-layouts: 7.4 us -> 5.52 us
    dynamic_slice x1 -> x0, local copies, waits for them, and re-layouts: 1.24 us -> none  [per_device_gathered(): mine = lax.dynamic_slice(block_expert, (lax.axis_index('expert'),), (1,))]
where the time goes in v2:
time: 54.9 us; the launch traced here: 54.6 us
  Pallas kernels  48.5 us (88%)
  local copies, waits for them, and re-layouts  5.52 us (10%)
  between operations  0.65 us (1%)
    pallas_call x1, Pallas kernels, per_device_gathered(): pl.pallas_call(functools.partial(fused_kernel, pieces), out_shape=(jax.Sh...  48.5 us
    unnamed x10, local copies, waits for them, and re-layouts  5.52 us

profile of v2, /device:TPU:0, one launch (start us, length us, event | category | flops | bytes accessed | tf_op | source)
XLA Modules:
  0.0 54.6 jit_solution(10075295604230128182)
XLA Ops:
  0.6 48.5 %layer_backward.1 = (bf16[4096,128]{1,0:T(8,128)(2,1)}, bf16[4096,128]{1,0:T(8,128)(2,1)}, bf16[128,4096]{1,0:T(8,128)(2,1)}, f32[8,128]{1,0:T(8,128)}) custom-call(s32[16]{0:T(128)} %expert_ref.1, s32[8,128]{1,0:T(8,128)} %bitcast.16, s32[8,128]{1,0:T(8,128)} %bitcast.17, bf16[128,4096]{1,0:T(8,128)(2,1)} %x_hbm.1, bf16[128,4096]{1,0:T(8,128)(2,1)} %dy_hbm.1, ...), custom_call_target="tpu_custom_call" | custom-call | tf_op jit(solution)/shard_map/layer_backward/pallas_call | solution.py:415
  49.1 0.0 copy-start.1
  49.1 2.4 %copy.16 = bf16[1,4096,128]{2,1,0:T(8,128)(2,1)} copy(bf16[1,4096,128]{2,1,0:T(8,128)(2,1)} %bitcast.11) | data formatting | bytes 2097152
  51.5 0.0 copy-done.1
  51.5 0.0 copy-start
  51.5 1.0 %copy.17 = bf16[1,4096,128]{2,1,0:T(8,128)(2,1)} copy(bf16[1,4096,128]{2,1,0:T(8,128)(2,1)S(1)} %bitcast.10) | data formatting | bytes 2097152
  52.4 0.6 %copy-done = bf16[128,4096]{1,0:T(8,128)(2,1)S(1)} copy-done((bf16[128,4096]{1,0:T(8,128)(2,1)S(1)}, bf16[128,4096]{1,0:T(8,128)(2,1)}, u32[]{:S(2)}) %copy-start) | copy-done | bytes 1048600
  53.1 0.0 copy-start.2
  53.1 1.0 %copy.18 = bf16[1,128,4096]{2,1,0:T(8,128)(2,1)} copy(bf16[1,128,4096]{2,1,0:T(8,128)(2,1)S(1)} %bitcast.9) | data formatting | bytes 2097152
  54.1 0.0 copy-done.2
  54.1 0.6 %copy.19 = f32[128,8]{0,1:T(8,128)} copy(f32[128,8]{0,1:T(8,128)S(1)} %bitcast.15) | data formatting | bytes 8192
Async XLA Ops:
  49.1 2.4 %copy-start.1 = (bf16[4096,128]{1,0:T(8,128)(2,1)S(1)}, bf16[4096,128]{1,0:T(8,128)(2,1)}, u32[]{:S(2)}) copy-start(bf16[4096,128]{1,0:T(8,128)(2,1)} %get-tuple-element.9) | copy-start | bytes 3145732
  51.5 1.6 %copy-start = (bf16[128,4096]{1,0:T(8,128)(2,1)S(1)}, bf16[128,4096]{1,0:T(8,128)(2,1)}, u32[]{:S(2)}) copy-start(bf16[128,4096]{1,0:T(8,128)(2,1)} %get-tuple-element.10) | copy-start | bytes 3145732
  53.1 1.0 %copy-start.2 = (f32[8,128]{1,0:T(8,128)S(1)}, f32[8,128]{1,0:T(8,128)}, u32[]{:S(2)}) copy-start(f32[8,128]{1,0:T(8,128)} %get-tuple-element.11) | copy-start | bytes 12292

commit v3 on v2

--- a/solution.py
+++ b/solution.py
@@ -142,6 +142,8 @@
     packed,
     grad_joined,
     grad_down,
+    sum_joined,
+    sum_down,
     dots,
     held,
     load_sem,
@@ -205,8 +207,11 @@
         else:
             pl.when(condition)(action)
 
+    def position(shard):
+        return lax.rem(shard // 2, 2) * (2 * depth) + (shard // 4) * 2 + lax.rem(shard, 2)
+
     def shard_rows(shard):
-        return pl.ds(pl.multiple_of(shard * ROWS, ROWS), ROWS)
+        return pl.ds(pl.multiple_of(position(shard) * ROWS, ROWS), ROWS)
 
     first, second, rest_hot, gain, slot = slot_tables(ids_ref[...], weight_ref[...])
     main = (first + second).astype(jnp.bfloat16)
@@ -282,35 +287,35 @@
 
         pl.when((z + shift >= 0) & (z + shift < depth))(lambda: each_piece(action))
 
-    def everything(method):
+    def early(method):
         own_sends(method)
-        for shift in range(1, depth + 1):
-            if shift < depth:
-                column_shard(-shift, 0, method)
-                column_shard(shift, 1, method)
+        for shift in range(1, depth):
+            column_shard(-shift, 0, method)
+            column_shard(shift, 1, method)
             if shift == 1:
                 across_shard(0, method)
-            else:
+            elif shift < depth - 1:
                 across_shard(1 - shift, method)
                 across_shard(shift - 1, method)
 
-    everything("start")
-
-    def sibling(number, carry):
-        each_piece(lambda piece: copy(number * 2 + 1 - core, piece, 3).wait_recv())
-        return carry
-
-    lax.fori_loop(0, depth * 2, sibling, 0)
-    for load in loads[2:]:
-        load.wait()
-
-    rows = packed.shape[0]
+    def late(method):
+        for shift in range(depth - 2, depth):
+            across_shard(-shift, method)
+            across_shard(shift, method)
+
+    def sibling(column):
+        def body(number, carry):
+            each_piece(lambda piece: copy(place(number, column, 1 - core), piece, 3).wait_recv())
+            return carry
+
+        lax.fori_loop(0, depth, body, 0)
+
+    count = packed.shape[0] // 2
     expert = expert_ref[me]
-    row_slot = lax.broadcasted_iota(jnp.int32, (rows, 1), 0) % ROWS
-    gains = packed[:, 2 * width + half :].astype(jnp.float32)
+    row_slot = lax.broadcasted_iota(jnp.int32, (count, 1), 0) % ROWS
     main_on = (row_slot >= CAP).astype(jnp.int32) == expert
     rest_on = (row_slot < 4) & (expert == 1)
-    rest = packed[:, 2 * width : 2 * width + half]
+    on = jnp.concatenate([main_on.astype(jnp.float32), rest_on.astype(jnp.float32)], axis=0) > 0.5
     across = (((1,), (1,)), ((), ()))
     down = (((0,), (0,)), ((), ()))
 
@@ -318,34 +323,11 @@
         return lax.dot_general(a, b, dims, preferred_element_type=jnp.float32)
 
     def up_rows(a, amount):
-        return pltpu.roll(a, rows - amount, 0)
-
-    pre_main = dot(packed[:, :width], joined_ref[...])
-    back_main = dot(packed[:, width : 2 * width], down_ref[...], across)
-    pre_rest = dot(rest, joined_ref[:half, :]) + up_rows(dot(rest, joined_ref[half:, :]), 4)
-    back_rest = up_rows(dot(rest, down_ref[:, :half], across), 8) + up_rows(
-        dot(rest, down_ref[:, half:], across), 12
-    )
-
-    def middle(pre, back, gain, on):
-        gain = jnp.where(on, gain, 0.0)
-        pre_gate, pre_up = pre[:, :blk], pre[:, blk:]
-        sigma = jax.nn.sigmoid(pre_gate)
-        hidden = (pre_gate * sigma * pre_up).astype(jnp.bfloat16).astype(jnp.float32)
-        products = jnp.where(on, jnp.sum(hidden * back, axis=1, keepdims=True), 0.0)
-        d_hidden = gain * back
-        d_gate = d_hidden * pre_up * sigma * (1.0 + pre_gate * (1.0 - sigma))
-        d_up = d_hidden * pre_gate * sigma
-        return products, gain * hidden, jnp.concatenate([d_gate, d_up], axis=1)
-
-    dots_main, scaled_main, d_main = middle(pre_main, back_main, gains[:, 0:1], main_on)
-    dots_rest, scaled_rest, d_rest = middle(pre_rest, back_rest, gains[:, 64:65], rest_on)
-    wide_lane = lax.broadcasted_iota(jnp.int32, (rows, 128), 1)
-    dots[...] = jnp.where(wide_lane < 64, dots_main, dots_rest).reshape(devices, ROWS, 128)
+        return pltpu.roll(a, count - amount, 0)
 
     def dot_copy(device, landing, sender):
         return pltpu.make_async_remote_copy(
-            src_ref=dots.at[device],
+            src_ref=dots.at[position(device)],
             dst_ref=held.at[landing],
             send_sem=dot_send.at[device],
             recv_sem=dot_recv.at[sender],
@@ -353,37 +335,94 @@
             device_id_type=MESH,
         )
 
-    each_other(lambda device: dot_copy(device, me, me).start())
-    held[me] = dots[me]
-
-    scaled = scaled_main.astype(jnp.bfloat16)
-    d_joined = d_main.astype(jnp.bfloat16)
-    stores = []
-    for part in range(2):
-        d_part = pltpu.roll(d_rest, 4 * part, 0) if part else d_rest
-        d_part = d_part.astype(jnp.bfloat16)
-        scaled_part = pltpu.roll(scaled_rest, 8 + 4 * part, 0).astype(jnp.bfloat16)
-        tile = 512
-        for start in range(0, half, tile):
-            here = slice(part * half + start, part * half + start + tile)
-            rest_here = packed[:, 2 * width + start : 2 * width + start + tile]
-            grad = dot(packed[:, here], d_joined, down) + dot(rest_here, d_part, down)
-            grad_joined[here, :] = grad.astype(jnp.bfloat16)
-            there = slice(width + here.start, width + here.stop)
-            grad_down[:, here] = (
-                dot(scaled, packed[:, there], down) + dot(scaled_part, rest_here, down)
+    def half_rows(column, finish):
+        rows = pl.ds(pl.multiple_of(column * count, count), count)
+        rest = packed[rows, 2 * width : 2 * width + half]
+
+        def stacked(start, size, rest_start):
+            return jnp.concatenate(
+                [packed[rows, start : start + size], rest[:, rest_start : rest_start + size]], axis=0
+            )
+
+        pre_low = dot(stacked(0, half, 0), joined_ref[:half, :])
+        pre_high = dot(stacked(half, half, 0), joined_ref[half:, :])
+        back_low = dot(stacked(width, half, 0), down_ref[:, :half], across)
+        back_high = dot(stacked(width + half, half, 0), down_ref[:, half:], across)
+        pre = jnp.concatenate(
+            [pre_low[:count] + pre_high[:count], pre_low[count:] + up_rows(pre_high[count:], 4)], axis=0
+        )
+        back = jnp.concatenate(
+            [
+                back_low[:count] + back_high[:count],
+                up_rows(back_low[count:], 8) + up_rows(back_high[count:], 12),
+            ],
+            axis=0,
+        )
+        gains = packed[rows, 2 * width + half :].astype(jnp.float32)
+        gain = jnp.where(on, jnp.concatenate([gains[:, 0:1], gains[:, 64:65]], axis=0), 0.0)
+        pre_gate, pre_up = pre[:, :blk], pre[:, blk:]
+        sigma = jax.nn.sigmoid(pre_gate)
+        hidden = (pre_gate * sigma * pre_up).astype(jnp.bfloat16).astype(jnp.float32)
+        products = jnp.where(on, jnp.sum(hidden * back, axis=1, keepdims=True), 0.0)
+        scaled = gain * hidden
+        d_hidden = gain * back
+        d_gate = d_hidden * pre_up * sigma * (1.0 + pre_gate * (1.0 - sigma))
+        d_up = d_hidden * pre_gate * sigma
+        d_joined = jnp.concatenate([d_gate, d_up], axis=1)
+        wide_lane = lax.broadcasted_iota(jnp.int32, (count, 128), 1)
+        dots[pl.ds(column * 2 * depth, 2 * depth)] = jnp.where(
+            wide_lane < 64, products[:count], products[count:]
+        ).reshape(2 * depth, ROWS, 128)
+
+        def send(number, carry):
+            device = place(number // 2, column, lax.rem(number, 2))
+            pl.when(device != me)(lambda: dot_copy(device, me, me).start())
+            return carry
+
+        lax.fori_loop(0, 2 * depth, send, 0)
+
+        stores = []
+        for part in range(2):
+            d_rest = pltpu.roll(d_joined[count:], 4 * part, 0) if part else d_joined[count:]
+            d_rows = jnp.concatenate([d_joined[:count], d_rest], axis=0).astype(jnp.bfloat16)
+            scaled_rows = jnp.concatenate(
+                [scaled[:count], pltpu.roll(scaled[count:], 8 + 4 * part, 0)], axis=0
             ).astype(jnp.bfloat16)
-        block = pl.ds(part * half, half)
-        for number, (source, target) in enumerate(
-            (
-                (grad_joined.at[block, 0:blk], gate_out.at[block, :]),
-                (grad_joined.at[block, blk : 2 * blk], up_out.at[block, :]),
-                (grad_down.at[:, block], down_out.at[:, block]),
-            )
-        ):
-            store = pltpu.make_async_copy(source, target, store_sem.at[part * 3 + number])
-            store.start()
-            stores.append(store)
+            tile = 512
+            for start in range(0, half, tile):
+                at = part * half + start
+                here = slice(at, at + tile)
+                grad = dot(stacked(at, tile, start), d_rows, down)
+                grad_d = dot(scaled_rows, stacked(width + at, tile, start), down)
+                if finish:
+                    grad_joined[here, :] = (sum_joined[here, :] + grad).astype(jnp.bfloat16)
+                    grad_down[:, here] = (sum_down[:, here] + grad_d).astype(jnp.bfloat16)
+                else:
+                    sum_joined[here, :] = grad
+                    sum_down[:, here] = grad_d
+            if finish:
+                block = pl.ds(part * half, half)
+                for number, (source, target) in enumerate(
+                    (
+                        (grad_joined.at[block, 0:blk], gate_out.at[block, :]),
+                        (grad_joined.at[block, blk : 2 * blk], up_out.at[block, :]),
+                        (grad_down.at[:, block], down_out.at[:, block]),
+                    )
+                ):
+                    store = pltpu.make_async_copy(source, target, store_sem.at[part * 3 + number])
+                    store.start()
+                    stores.append(store)
+        return stores
+
+    early("start")
+    for load in loads[2:]:
+        load.wait()
+    sibling(y)
+    half_rows(y, False)
+    held[me] = dots[position(me)]
+    late("start")
+    sibling(1 - y)
+    stores = half_rows(1 - y, True)
 
     each_other(lambda device: dot_copy(device, device, device).wait_recv())
     total = held[0]
@@ -396,7 +435,30 @@
     high = jnp.sum(second * total_main + jnp.where(slot < 4, rest_hot * extra, 0.0), axis=0, keepdims=True)
     route_out[...] = jnp.where(ids == 0, low, jnp.where(ids == 1, high, 0.0))
     each_other(lambda device: dot_copy(device, me, me).wait_send())
-    everything("wait_send")
+    early("wait_send")
+    late("wait_send")
+    for store in stores:
+        store.wait()
+
+
+def write_kernel(a_in, b_in, c_in, route_in, a_out, b_out, c_out, route_out, a, b, c, load_sem, store_sem):
+    loads, stores = [], []
+    for number, (source, through, target) in enumerate(((a_in, a, a_out), (b_in, b, b_out), (c_in, c, c_out))):
+        rows = source.shape[0] // 2
+        for part in range(2):
+            block = pl.ds(part * rows, rows)
+            loads.append(
+                pltpu.make_async_copy(source.at[block], through.at[block], load_sem.at[number, part])
+            )
+            stores.append(
+                pltpu.make_async_copy(through.at[block], target.at[block], store_sem.at[number, part])
+            )
+    for load in loads:
+        load.start()
+    route_out[...] = route_in[...]
+    for load, store in zip(loads, stores):
+        load.wait()
+        store.start()
     for store in stores:
         store.wait()
 
@@ -430,6 +492,8 @@
             pltpu.VMEM((devices * ROWS, total), jnp.bfloat16),
             pltpu.VMEM((width, 2 * blk), jnp.bfloat16),
             pltpu.VMEM((blk, width), jnp.bfloat16),
+            pltpu.VMEM((width, 2 * blk), jnp.float32),
+            pltpu.VMEM((blk, width), jnp.float32),
             pltpu.VMEM((devices, ROWS, 128), jnp.float32),
             pltpu.VMEM((devices, ROWS, 128), jnp.float32),
             pltpu.SemaphoreType.DMA((5,)),
@@ -444,6 +508,17 @@
         ),
         name="layer_backward",
     )(block_expert, ids, weights, tokens, grad_out, gate_blocks[0], up_blocks[0], down_blocks[0])
+    results = (grad_gate, grad_up, grad_down)
+    grad_gate, grad_up, grad_down, route_grad = pl.pallas_call(
+        write_kernel,
+        out_shape=tuple(jax.ShapeDtypeStruct(a.shape, a.dtype) for a in (*results, route_grad)),
+        in_specs=[anywhere] * 3 + [vmem],
+        out_specs=(anywhere,) * 3 + (vmem,),
+        scratch_shapes=[pltpu.VMEM(a.shape, a.dtype) for a in results]
+        + [pltpu.SemaphoreType.DMA((3, 2)), pltpu.SemaphoreType.DMA((3, 2))],
+        compiler_params=pltpu.CompilerParams(vmem_limit_bytes=58 * 1024 * 1024),
+        name="write_results",
+    )(*results, route_grad)
     return (grad_gate[None], grad_up[None], grad_down[None], route_grad.T)
 
 

time: 54.9 us -> 52.6 us (0.958)
  local copies, waits for them, and re-layouts: 5.52 us -> 0 us
  Pallas kernels: 48.5 us -> 51.7 us
    unnamed x10 -> x0, local copies, waits for them, and re-layouts: 5.52 us -> none
    pallas_call x0 -> x1, Pallas kernels: none -> 4.08 us  [per_device_gathered(): pl.pallas_call(write_kernel, out_shape=tuple((jax.ShapeDtypeStruct(a.shap...]
    pallas_call x1, Pallas kernels: 48.5 us -> 47.7 us  [per_device_gathered(): pl.pallas_call(functools.partial(fused_kernel, pieces), out_shape=(jax.Sh...]
where the time goes in v3:
time: 52.6 us; the launch traced here: 52.4 us
  Pallas kernels  51.7 us (98%)
  between operations  0.64 us (1%)
    pallas_call x1, Pallas kernels, per_device_gathered(): pl.pallas_call(functools.partial(fused_kernel, pieces), out_shape=(jax.Sh...  47.7 us
    pallas_call x1, Pallas kernels, per_device_gathered(): pl.pallas_call(write_kernel, out_shape=tuple((jax.ShapeDtypeStruct(a.shap...  4.08 us

profile of v3, /device:TPU:0, one launch (start us, length us, event | category | flops | bytes accessed | tf_op | source)
XLA Modules:
  0.0 52.4 jit_solution(2110670109874164271)
XLA Ops:
  0.6 47.7 %layer_backward.1 = (bf16[4096,128]{1,0:T(8,128)(2,1)}, bf16[4096,128]{1,0:T(8,128)(2,1)}, bf16[128,4096]{1,0:T(8,128)(2,1)}, f32[8,128]{1,0:T(8,128)}) custom-call(s32[16]{0:T(128)} %expert_ref.1, s32[8,128]{1,0:T(8,128)} %bitcast.12, s32[8,128]{1,0:T(8,128)} %bitcast.13, bf16[128,4096]{1,0:T(8,128)(2,1)} %x_hbm.1, bf16[128,4096]{1,0:T(8,128)(2,1)} %dy_hbm.1, ...), custom_call_target="tpu_custom_call" | custom-call | tf_op jit(solution)/shard_map/layer_backward/pallas_call | solution.py:477
  48.3 4.1 %write_results.1 = (bf16[4096,128]{1,0:T(8,128)(2,1)}, bf16[4096,128]{1,0:T(8,128)(2,1)}, bf16[128,4096]{1,0:T(8,128)(2,1)}, f32[8,128]{1,0:T(8,128)}) custom-call(bf16[4096,128]{1,0:T(8,128)(2,1)} %get-tuple-element.12.a_in, bf16[4096,128]{1,0:T(8,128)(2,1)} %get-tuple-element.13.b_in, bf16[128,4096]{1,0:T(8,128)(2,1)} %get-tuple-element.14.c_in, ...), custom_call_target="tpu_custom_call" | custom-call | tf_op jit(solution)/shard_map/write_results/pallas_call | solution.py:512

commit v4 on v3

--- a/solution.py
+++ b/solution.py
@@ -161,7 +161,6 @@
     blk = down_ref.shape[0]
     half = width // 2
     step = packed.shape[1] // pieces
-    last = pieces - 1
 
     loads = [
         pltpu.make_async_copy(source, target, load_sem.at[number])
@@ -199,7 +198,6 @@
         (place(z, 1 - y, core), None),
         (place(z, y, 1 - core), None),
     )
-    partner = z + 1 - 2 * (z % 2)
 
     def under(condition, action):
         if condition is None:
@@ -222,19 +220,6 @@
     packed[mine, 2 * width + half :] = jnp.where(lane < 64, main_gain, rest_gain).astype(jnp.bfloat16)
     loads[0].wait()
     packed[mine, 0:width] = jnp.dot(main, x_ref[...], preferred_element_type=jnp.float32).astype(jnp.bfloat16)
-    loads[1].wait()
-    packed[mine, width : 2 * width] = jnp.dot(main, dy_ref[...], preferred_element_type=jnp.float32).astype(
-        jnp.bfloat16
-    )
-    total = jnp.zeros((ROWS, half), jnp.float32)
-    for quarter in range(4):
-        chosen = jnp.where(slot // 4 == quarter, rest_hot, 0.0).astype(jnp.bfloat16)
-        source = x_ref if quarter < 2 else dy_ref
-        total = total + jnp.dot(
-            chosen, source[:, (quarter % 2) * half : (quarter % 2 + 1) * half], preferred_element_type=jnp.float32
-        )
-    packed[mine, 2 * width : 2 * width + half] = total.astype(jnp.bfloat16)
-
     pl.semaphore_wait(barrier, devices - 1)
 
     def copy(shard, piece, way):
@@ -255,12 +240,25 @@
 
         lax.fori_loop(0, pieces, body, 0)
 
-    def own_sends(method):
-        def action(piece):
-            for way in (2, 0, 1, 3):
-                under(targets[way][1], lambda way=way: getattr(copy(me, piece, way), method)())
-
-        each_piece(action)
+    def own_piece(piece, method):
+        for way in (2, 0, 1, 3):
+            under(targets[way][1], lambda way=way: getattr(copy(me, piece, way), method)())
+
+    own_piece(0, "start")
+    loads[1].wait()
+    packed[mine, width : 2 * width] = jnp.dot(main, dy_ref[...], preferred_element_type=jnp.float32).astype(
+        jnp.bfloat16
+    )
+    total = jnp.zeros((ROWS, half), jnp.float32)
+    for quarter in range(4):
+        chosen = jnp.where(slot // 4 == quarter, rest_hot, 0.0).astype(jnp.bfloat16)
+        source = x_ref if quarter < 2 else dy_ref
+        total = total + jnp.dot(
+            chosen, source[:, (quarter % 2) * half : (quarter % 2 + 1) * half], preferred_element_type=jnp.float32
+        )
+    packed[mine, 2 * width : 2 * width + half] = total.astype(jnp.bfloat16)
+    for piece in range(1, pieces):
+        own_piece(piece, "start")
 
     def column_shard(shift, way, method):
         shard = place(z + shift, y, core)
@@ -269,7 +267,7 @@
             if method == "start":
                 copy(shard, piece, 2).wait_recv()
             under(targets[way][1], lambda: getattr(copy(shard, piece, way), method)())
-            pl.when((piece < last) | (z + shift != partner))(lambda: getattr(copy(shard, piece, 2), method)())
+            getattr(copy(shard, piece, 2), method)()
             getattr(copy(shard, piece, 3), method)()
 
         pl.when((z + shift >= 0) & (z + shift < depth))(lambda: each_piece(action))
@@ -280,15 +278,11 @@
         def action(piece):
             if method == "start":
                 copy(shard, piece, 3).wait_recv()
-            if shift == 0:
-                pl.when((piece == last) & (z % 2 == 0))(lambda: getattr(copy(shard, piece, 0), method)())
-                pl.when((piece == last) & (z % 2 == 1))(lambda: getattr(copy(shard, piece, 1), method)())
             getattr(copy(shard, piece, 3), method)()
 
         pl.when((z + shift >= 0) & (z + shift < depth))(lambda: each_piece(action))
 
     def early(method):
-        own_sends(method)
         for shift in range(1, depth):
             column_shard(-shift, 0, method)
             column_shard(shift, 1, method)
@@ -435,6 +429,8 @@
     high = jnp.sum(second * total_main + jnp.where(slot < 4, rest_hot * extra, 0.0), axis=0, keepdims=True)
     route_out[...] = jnp.where(ids == 0, low, jnp.where(ids == 1, high, 0.0))
     each_other(lambda device: dot_copy(device, me, me).wait_send())
+    for piece in range(pieces):
+        own_piece(piece, "wait_send")
     early("wait_send")
     late("wait_send")
     for store in stores:

time: 52.6 us -> 51.7 us (0.983)
  Pallas kernels: 51.7 us -> 50.8 us
    pallas_call x1, Pallas kernels: 47.7 us -> 46.7 us  [per_device_gathered(): pl.pallas_call(functools.partial(fused_kernel, pieces), out_shape=(jax.Sh...]
where the time goes in v4:
time: 51.7 us; the launch traced here: 51.4 us
  Pallas kernels  50.8 us (98%)
  between operations  0.64 us (1%)
    pallas_call x1, Pallas kernels, per_device_gathered(): pl.pallas_call(functools.partial(fused_kernel, pieces), out_shape=(jax.Sh...  46.7 us
    pallas_call x1, Pallas kernels, per_device_gathered(): pl.pallas_call(write_kernel, out_shape=tuple((jax.ShapeDtypeStruct(a.shap...  4.08 us

profile of v4, /device:TPU:0, one launch (start us, length us, event | category | flops | bytes accessed | tf_op | source)
XLA Modules:
  0.0 51.4 jit_solution(2166713893713615816)
XLA Ops:
  0.6 46.7 %layer_backward.1 = (bf16[4096,128]{1,0:T(8,128)(2,1)}, bf16[4096,128]{1,0:T(8,128)(2,1)}, bf16[128,4096]{1,0:T(8,128)(2,1)}, f32[8,128]{1,0:T(8,128)}) custom-call(s32[16]{0:T(128)} %expert_ref.1, s32[8,128]{1,0:T(8,128)} %bitcast.12, s32[8,128]{1,0:T(8,128)} %bitcast.13, bf16[128,4096]{1,0:T(8,128)(2,1)} %x_hbm.1, bf16[128,4096]{1,0:T(8,128)(2,1)} %dy_hbm.1, ...), custom_call_target="tpu_custom_call" | custom-call | tf_op jit(solution)/shard_map/layer_backward/pallas_call | solution.py:473
  47.4 4.1 %write_results.1 = (bf16[4096,128]{1,0:T(8,128)(2,1)}, bf16[4096,128]{1,0:T(8,128)(2,1)}, bf16[128,4096]{1,0:T(8,128)(2,1)}, f32[8,128]{1,0:T(8,128)}) custom-call(bf16[4096,128]{1,0:T(8,128)(2,1)} %get-tuple-element.12.a_in, bf16[4096,128]{1,0:T(8,128)(2,1)} %get-tuple-element.13.b_in, bf16[128,4096]{1,0:T(8,128)(2,1)} %get-tuple-element.14.c_in, ...), custom_call_target="tpu_custom_call" | custom-call | tf_op jit(solution)/shard_map/write_results/pallas_call | solution.py:508
